TPU v7x, 128 devices: a whole 4x4x4 slice. The times are simulated.
128 devices in a mesh: xy: 32 (over x, y, core), gz: 4 (over z).
Axes of the slice: x: 4, y: 4, z: 4, core: 2. Of those that a mesh axis runs over, the one named last changes fastest.
Arguments:
- estimate: float32 [512, 64, 512], P('xy', None, 'gz'), may hold values from 0.25 to 4
- observed: float32 [6, 512, 64, 512], P(None, None, 'xy', 'gz'), may hold values from 0.2 to 5
- kernels: float32 [6, 3, 15], replicated, may hold values from 0.05 to 1
- view_shift: int32 [6], replicated, may hold values from -16 to 16
Outputs:
- updated: float32 [512, 64, 512], P('xy', None, 'gz')
All inputs are finite; a program needn't handle non-finite values.
Results may differ from a plain program's by a relative error of at most 0.0001.
Values sent between devices are 32-bit elements; how exact they have to be, the bound alone decides.
A program may use at most 128 MiB of HBM per device.

v0:
```python
import functools

import jax
import jax.numpy as jnp
from jax import lax
from jax.experimental import pallas as pl
from jax.experimental.pallas import tpu as pltpu
from jax.sharding import PartitionSpec as P

MESH = pl.DeviceIdType.MESH
F32, BF16 = jnp.float32, jnp.bfloat16
TAPS, HALF = 15, 7
SIDES = ((-1, 0), (1, 0), (0, -1), (0, 1), (-1, -1), (-1, 1), (1, -1), (1, 1))


def split(a):
    high = a.astype(BF16)
    return high, (a - high.astype(F32)).astype(BF16)


def dot3(a, b, dims):
    (ah, al), (bh, bl) = a, b
    one = lambda p, q: lax.dot_general(p, q, (dims, ((), ())), preferred_element_type=F32)
    return one(ah, bh) + (one(al, bh) + one(ah, bl))


NN = ((1,), (0,))
NT = ((1,), (1,))
TN = ((0,), (0,))


def kernel(n, depth, views, taps_ref, shift_ref, est_ref, obs_ref, out_ref, *scratch):
    tiles = scratch[:views]
    (field, halo_z, zed, xed, blurs, ratio, yed, spread, total, spill, got_x, got_z,
     w_main, w_back, w_side,
     a2a_send, a2a_recv, own_sem, halo_send, halo_recv, spill_send, spill_recv) = scratch[views:]
    rows = 2 * n
    slab = rows * 8
    me, deep = lax.axis_index("xy"), lax.axis_index("gz")

    def peer(side):
        return {"xy": lax.rem(me + side[0] + n, n), "gz": lax.rem(deep + side[1] + depth, depth)}

    barrier = pltpu.get_barrier_semaphore()

    def greet(k, carry):
        pl.semaphore_signal(barrier, inc=1, device_id={"xy": lax.rem(me + k, n)}, device_id_type=MESH)
        return carry

    lax.fori_loop(1, n, greet, 0)
    for side in SIDES[2:]:
        pl.semaphore_signal(barrier, inc=1, device_id=peer(side), device_id_type=MESH)

    def arrange(y, carry):
        for t in range(2):
            field[1 + t, y] = est_ref[pl.ds(t * 8 * rows + y, 8, stride=rows), :]
        return carry

    lax.fori_loop(0, rows, arrange, 0)
    for t in range(2):
        turned = field[1 + t].reshape(slab, 128).T
        spill[0, 1 + t] = turned[0:8]
        spill[1, 1 + t] = turned[120:128]
    pl.semaphore_wait(barrier, n - 1 + 6)

    def halo_copies():
        out = []
        for i, (sx, sz) in enumerate(SIDES):
            if sz == 0:
                src = field.at[1 if sx < 0 else 2]
                dst = field.at[3 if sx < 0 else 0]
            else:
                mine, theirs = (0, 1) if sz < 0 else (1, 0)
                if sx == 0:
                    src, dst = spill.at[mine, pl.ds(1, 2)], halo_z.at[theirs, pl.ds(1, 2)]
                else:
                    src = spill.at[mine, 1 if sx < 0 else 2]
                    dst = halo_z.at[theirs, 3 if sx < 0 else 0]
            out.append(pltpu.make_async_remote_copy(
                src_ref=src, dst_ref=dst, send_sem=halo_send.at[i], recv_sem=halo_recv.at[i],
                device_id=peer((sx, sz)), device_id_type=MESH))
        return out

    halos = halo_copies()
    for copy in halos:
        copy.start()

    for v in range(views):
        def send(k, carry, v=v):
            to = lax.rem(me + k, n)
            pltpu.make_async_remote_copy(
                src_ref=obs_ref.at[v, pl.ds(pl.multiple_of(to * 32, 32), 32)],
                dst_ref=tiles[v].at[me],
                send_sem=a2a_send.at[v], recv_sem=a2a_recv.at[v],
                device_id={"xy": to}, device_id_type=MESH).start()
            return carry

        lax.fori_loop(1, n, send, 0)
        pltpu.make_async_copy(
            obs_ref.at[v, pl.ds(pl.multiple_of(me * 32, 32), 32)], tiles[v].at[me], own_sem.at[v]).start()

    def tap(v, axis, t):
        return taps_ref[(v * 3 + axis) * TAPS + t]

    def banded(v, tap_at):
        band = jnp.zeros(tap_at.shape, F32)
        for t in range(TAPS):
            band = jnp.where(tap_at == t, tap(v, 2, t), band)
        return band

    def build(v, carry):
        row = lax.broadcasted_iota(jnp.int32, (128, 128), 0)
        col = lax.broadcasted_iota(jnp.int32, (128, 128), 1)
        w_main[v, 0], w_main[v, 1] = split(banded(v, row - col + HALF))
        w_back[v, 0], w_back[v, 1] = split(banded(v, col - row + HALF))
        row = lax.broadcasted_iota(jnp.int32, (16, 128), 0)
        col = lax.broadcasted_iota(jnp.int32, (16, 128), 1)
        place = jnp.where(row < 8, row - 8, row + 120)
        w_side[v, 0], w_side[v, 1] = split(banded(v, place - col + HALF))
        return carry

    lax.fori_loop(0, views, build, 0)
    xed[0:8] = jnp.zeros((8, 16, 128), F32)
    xed[rows + 8:rows + 16] = jnp.zeros((8, 16, 128), F32)
    ratio[0:8] = jnp.zeros((8, 16, 128), F32)
    ratio[rows + 8:rows + 16] = jnp.zeros((8, 16, 128), F32)
    yed[:, 0:8] = jnp.zeros((rows, 8, 128), F32)
    yed[:, 24:32] = jnp.zeros((rows, 8, 128), F32)

    for copy in halos:
        copy.wait_recv()
    first, last = me == 0, me == n - 1
    front, rear = deep == 0, deep == depth - 1
    field[0] = jnp.where(first, 0.0, field[0])
    field[3] = jnp.where(last, 0.0, field[3])
    halo_z[0] = jnp.where(front, 0.0, halo_z[0])
    halo_z[1] = jnp.where(rear, 0.0, halo_z[1])
    for side in range(2):
        halo_z[side, 0] = jnp.where(first, 0.0, halo_z[side, 0])
        halo_z[side, 3] = jnp.where(last, 0.0, halo_z[side, 3])

    def along_y(taps, src, put):
        def block(b, carry):
            for t in range(2):
                sums = [None] * 8
                for r in range(22):
                    seen = src[b * 8 + 1 + r, pl.ds(t * 8, 8), :]
                    for j in range(max(0, r - 14), min(8, r + 1)):
                        term = taps[r - j] * seen
                        sums[j] = term if sums[j] is None else sums[j] + term
                for j in range(8):
                    put(b * 8 + j, t, sums[j])
            return carry

        lax.fori_loop(0, rows // 8, block, 0)

    def forward(v, carry):
        main, side = (w_main[v, 0], w_main[v, 1]), (w_side[v, 0], w_side[v, 1])
        for t in range(4):
            res = dot3(split(field[t].reshape(slab, 128)), main, NN)
            ends = jnp.concatenate([halo_z[0, t], halo_z[1, t]], axis=0)
            res = res + dot3(split(ends), side, TN)
            zed[:, t * 8:t * 8 + 8, :] = res.reshape(rows, 8, 128)
        taps = [jnp.full((8, 128), tap(v, 0, t), F32) for t in range(TAPS)]

        def along_x(y, c):
            low = high = None
            for o in range(1, 24):
                seen = zed[y, pl.ds(o, 8), :]
                if o <= 15:
                    term = taps[o - 1] * seen
                    low = term if low is None else low + term
                if o >= 9:
                    term = taps[o - 9] * seen
                    high = term if high is None else high + term
            xed[y + 8, 0:8, :] = low
            xed[y + 8, 8:16, :] = high
            return c

        lax.fori_loop(0, rows, along_x, 0, unroll=4)
        taps_y = [jnp.full((8, 128), tap(v, 1, t), F32) for t in range(TAPS)]

        def put(y, t, value):
            blurs[v, y, pl.ds(t * 8, 8), :] = value

        along_y(taps_y, xed, put)
        return carry

    lax.fori_loop(0, views, forward, 0)

    def backward(v):
        shift = shift_ref[v]
        whole = tiles[v].at[pl.ds(0, n - 1)]
        pltpu.make_async_copy(whole, whole, a2a_recv.at[v]).wait()
        pltpu.make_async_copy(
            obs_ref.at[v, pl.ds(pl.multiple_of(me * 32, 32), 32)], tiles[v].at[me], own_sem.at[v]).wait()
        flat = tiles[v].reshape(n * 32, 128)

        def divide(y, carry):
            at = y + shift
            inside = jnp.clip(at, 0, rows - 1)
            base = (inside // 2) * 32 + inside % 2
            covered = jnp.logical_and(at >= 0, at < rows)
            for t in range(2):
                seen = flat[pl.ds(base + t * 16, 8, stride=2), :]
                ratio[y + 8, pl.ds(t * 8, 8), :] = jnp.where(
                    covered, seen / blurs[v, y, pl.ds(t * 8, 8), :], jnp.float32(1.0))
            return carry

        lax.fori_loop(0, rows, divide, 0, unroll=4)
        taps_y = [jnp.full((8, 128), tap(v, 1, TAPS - 1 - t), F32) for t in range(TAPS)]

        def put(y, t, value):
            yed[y, pl.ds(8 + t * 8, 8), :] = value

        along_y(taps_y, ratio, put)
        taps = [jnp.full((8, 128), tap(v, 0, TAPS - 1 - t), F32) for t in range(TAPS)]

        def along_x(y, c):
            sums = [None] * 4
            for o in range(1, 24):
                seen = yed[y, pl.ds(o, 8), :]
                for j in range(4):
                    t = o + 7 - 8 * j
                    if 0 <= t < TAPS:
                        term = taps[t] * seen
                        sums[j] = term if sums[j] is None else sums[j] + term
            for j in range(4):
                spread[j, y] = sums[j]
            return c

        lax.fori_loop(0, rows, along_x, 0, unroll=2)
        main, side = (w_back[v, 0], w_back[v, 1]), (w_side[v, 0], w_side[v, 1])
        for t in range(4):
            parts = split(spread[t].reshape(slab, 128))
            res = dot3(parts, main, NN).reshape(rows, 8, 128)
            ends = dot3(side, parts, NT)
            if v == 0:
                total[t] = res
                spill[0, t], spill[1, t] = ends[0:8], ends[8:16]
            else:
                total[t] += res
                spill[0, t] += ends[0:8]
                spill[1, t] += ends[8:16]

    for copy in halos:
        copy.wait_send()
    for v in range(views):
        backward(v)

    spills = []
    for i, (sx, sz) in enumerate(SIDES):
        if sz == 0:
            src, dst = total.at[0 if sx < 0 else 3], got_x.at[1 if sx < 0 else 0]
        else:
            mine, theirs = (0, 1) if sz < 0 else (1, 0)
            if sx == 0:
                src, dst = spill.at[mine, pl.ds(1, 2)], got_z.at[theirs, pl.ds(1, 2)]
            else:
                src = spill.at[mine, 0 if sx < 0 else 3]
                dst = got_z.at[theirs, 3 if sx < 0 else 0]
        spills.append(pltpu.make_async_remote_copy(
            src_ref=src, dst_ref=dst, send_sem=spill_send.at[i], recv_sem=spill_recv.at[i],
            device_id=peer((sx, sz)), device_id_type=MESH))
    for copy in spills:
        copy.start()
    for v in range(views):
        whole = tiles[v].at[pl.ds(0, n - 1)]
        pltpu.make_async_copy(whole, whole, a2a_send.at[v]).wait()
    for copy in spills:
        copy.wait_recv()

    lane = lax.broadcasted_iota(jnp.int32, (16, 128), 1)
    row = lax.broadcasted_iota(jnp.int32, (16, 128), 0)
    place = jnp.where(lane == jnp.where(row < 8, row, row + 112), 1.0, 0.0).astype(BF16)
    for t in range(2):
        outer, edge = (0, first) if t == 0 else (1, last)
        corner = 0 if t == 0 else 3
        ends = []
        for side, face in ((0, front), (1, rear)):
            end = got_z[side, 1 + t] + jnp.where(edge, 0.0, got_z[side, corner])
            ends.append(jnp.where(face, 0.0, end))
        eh, el = split(jnp.concatenate(ends, axis=0))
        one = lambda p: lax.dot_general(p, place, (TN, ((), ())), preferred_element_type=F32)
        spilled = (one(eh) + one(el)).reshape(rows, 8, 128)
        summed = total[1 + t] + jnp.where(edge, 0.0, got_x[outer]) + spilled
        spread[t] = field[1 + t] * summed / views

    def finish(y, carry):
        for t in range(2):
            out_ref[pl.ds(t * 8 * rows + y, 8, stride=rows), :] = spread[t, y]
        return carry

    lax.fori_loop(0, rows, finish, 0)
    for copy in spills:
        copy.wait_send()


def local(n, depth, estimate, observed, kernels, view_shift):
    views, nx = observed.shape[:2]
    rows = estimate.shape[1]
    taps = (kernels / jnp.sum(kernels, axis=2, keepdims=True)).reshape(-1)
    est = estimate.reshape(16 * rows, 128)
    obs = observed.reshape(views, 2 * nx, 128)
    dma = pltpu.SemaphoreType.DMA
    vmem = lambda *shape: pltpu.VMEM(shape, F32)
    wide = lambda *shape: pltpu.VMEM(shape, BF16)
    out = pl.pallas_call(
        functools.partial(kernel, n, depth, views),
        out_shape=jax.ShapeDtypeStruct((16 * rows, 128), F32),
        in_specs=[
            pl.BlockSpec(memory_space=pltpu.SMEM),
            pl.BlockSpec(memory_space=pltpu.SMEM),
            pl.BlockSpec(memory_space=pltpu.VMEM),
            pl.BlockSpec(memory_space=pl.ANY),
        ],
        out_specs=pl.BlockSpec(memory_space=pltpu.VMEM),
        scratch_shapes=[vmem(n, 32, 128)] * views + [
            vmem(4, rows, 8, 128),
            vmem(2, 4, 8, rows * 8),
            vmem(rows, 32, 128),
            vmem(rows + 16, 16, 128),
            vmem(views, rows, 16, 128),
            vmem(rows + 16, 16, 128),
            vmem(rows, 32, 128),
            vmem(4, rows, 8, 128),
            vmem(4, rows, 8, 128),
            vmem(2, 4, 8, rows * 8),
            vmem(2, rows, 8, 128),
            vmem(2, 4, 8, rows * 8),
            wide(views, 2, 128, 128),
            wide(views, 2, 128, 128),
            wide(views, 2, 16, 128),
            dma((views,)), dma((views,)), dma((views,)),
            dma((8,)), dma((8,)), dma((8,)), dma((8,)),
        ],
        compiler_params=pltpu.CompilerParams(
            collective_id=0, has_side_effects=True, vmem_limit_bytes=56 * 2**20),
    )(taps, view_shift, est, obs)
    return out.reshape(estimate.shape)


def solution(mesh):
    return jax.shard_map(
        functools.partial(local, mesh.shape["xy"], mesh.shape["gz"]),
        mesh=mesh,
        in_specs=(P("xy", None, "gz"), P(None, None, "xy", "gz"), P(), P()),
        out_specs=P("xy", None, "gz"),
        check_vma=False,
    )
```

profile of v0, /device:TPU:23, one launch (start us, length us, event | category | flops | bytes accessed | tf_op | source)
XLA Modules:
  0.0 86.0 jit_solution(13031416958547307889)
XLA Ops:
  0.0 0.9 %fusion.1 = f32[6,3,15]{2,1,0:T(4,128)S(1)} fusion(f32[6,3,15]{2,1,0:T(4,128)} %param.6), kind=kOutput, calls=%fused_computation.1 | output fusion | flops 302 | bytes 2160 | tf_op jit(solution)/shard_map/div | solution.py:302
  0.9 0.7 reshape.13.taps_ref
  1.6 82.5 %shard_map.46 = f32[1024,128]{1,0:T(8,128)} custom-call(f32[270]{0:T(512)} %reshape.13.taps_ref, s32[6]{0:T(128)} %shift_ref.1, f32[1024,128]{1,0:T(8,128)} %bitcast.6, f32[6,1024,128]{2,1,0:T(8,128)} %bitcast.4), custom_call_target="tpu_custom_call" | custom-call | tf_op jit(solution)/shard_map/pallas_call | solution.py:308
  84.1 1.9 %copy.6 = f32[16,64,128]{2,1,0:T(8,128)} copy(f32[16,64,128]{2,1,0:T(8,128)} %bitcast.5) | data formatting | bytes 1048576
where the time goes:
time: 86.2 us; the launch traced here: 86 us
  Pallas kernels  82.5 us (96%)
  local copies, waits for them, and re-layouts  2.56 us (3%)
  other arithmetic  0.87 us (1%)
    pallas_call x1, Pallas kernels, local(): pl.pallas_call(functools.partial(kernel, n, depth, views), out_shape=jax....  82.5 us
    unnamed x1, local copies, waits for them, and re-layouts  1.89 us

commit v1 on v0

v1 whole, which is shorter than its diff:
```python
import functools

import jax
import jax.numpy as jnp
from jax import lax
from jax.experimental import pallas as pl
from jax.experimental.pallas import tpu as pltpu
from jax.sharding import PartitionSpec as P

MESH = pl.DeviceIdType.MESH
F32, BF16 = jnp.float32, jnp.bfloat16
TAPS, HALF = 15, 7
SIDES = ((-1, 0), (1, 0), (0, -1), (0, 1), (-1, -1), (-1, 1), (1, -1), (1, 1))


def split(a):
    high = a.astype(BF16)
    return high, (a - high.astype(F32)).astype(BF16)


def dot(a, b, dims):
    return lax.dot_general(a, b, (dims, ((), ())), preferred_element_type=F32)


NN = ((1,), (0,))
NT = ((1,), (1,))
TN = ((0,), (0,))
CHUNK = 16


def kernel(n, depth, views, kernels_ref, shift_ref, est_ref, obs_ref, out_ref,
           est, tiles, lined, field, wide, halo_z, zed, xed, weights, ratio, yed, spread, total, spill,
           got_x, got_z, w_fore, w_back, w_low, w_side,
           est_sem, a2a_send, a2a_recv, own_sem, halo_send, halo_recv, spill_send, spill_recv,
           chunk_send, chunk_recv):
    rows = 2 * n
    slab = rows * 8
    chunks = rows // CHUNK
    me, deep = lax.axis_index("xy"), lax.axis_index("gz")
    load = pltpu.make_async_copy(est_ref, est, est_sem)
    load.start()

    def peer(side):
        return {"xy": lax.rem(me + side[0] + n, n), "gz": lax.rem(deep + side[1] + depth, depth)}

    barrier = pltpu.get_barrier_semaphore()

    def greet(k, carry):
        pl.semaphore_signal(barrier, inc=1, device_id={"xy": lax.rem(me + k, n)}, device_id_type=MESH)
        return carry

    lax.fori_loop(1, n, greet, 0)
    for side in SIDES[2:]:
        pl.semaphore_signal(barrier, inc=1, device_id=peer(side), device_id_type=MESH)

    def own(v, wait):
        copy = pltpu.make_async_copy(
            obs_ref.at[v, pl.ds(pl.multiple_of(me * 32, 32), 32)], tiles.at[v, me], own_sem.at[v])
        copy.wait() if wait else copy.start()

    for v in range(views):
        own(v, False)

    load.wait()

    def arrange(y, carry):
        for t in range(2):
            field[1 + t, y] = est[pl.ds(t * 8 * rows + y, 8, stride=rows), :]
        return carry

    lax.fori_loop(0, rows, arrange, 0, unroll=8)
    for t in range(2):
        turned = field[1 + t].reshape(slab, 128).T
        spill[0, 1 + t] = turned[0:8]
        spill[1, 1 + t] = turned[120:128]
    pl.semaphore_wait(barrier, n - 1 + 6)

    halos = []
    for i, (sx, sz) in enumerate(SIDES):
        if sz == 0:
            src = field.at[1 if sx < 0 else 2]
            dst = field.at[3 if sx < 0 else 0]
        else:
            mine, theirs = (0, 1) if sz < 0 else (1, 0)
            if sx == 0:
                src, dst = spill.at[mine, pl.ds(1, 2)], halo_z.at[theirs, pl.ds(1, 2)]
            else:
                src = spill.at[mine, 1 if sx < 0 else 2]
                dst = halo_z.at[theirs, 3 if sx < 0 else 0]
        halos.append(pltpu.make_async_remote_copy(
            src_ref=src, dst_ref=dst, send_sem=halo_send.at[i], recv_sem=halo_recv.at[i],
            device_id=peer((sx, sz)), device_id_type=MESH))
    for copy in halos:
        copy.start()

    def send(v, k):
        to = lax.rem(me + k, n)
        pltpu.make_async_remote_copy(
            src_ref=obs_ref.at[v, pl.ds(pl.multiple_of(to * 32, 32), 32)],
            dst_ref=tiles.at[v, me],
            send_sem=a2a_send.at[v], recv_sem=a2a_recv.at[v],
            device_id={"xy": to}, device_id_type=MESH).start()

    def send_first(k, carry):
        send(0, k)
        return carry

    lax.fori_loop(1, n, send_first, 0)

    def paced(group, body, steps):
        if group is None:
            lax.fori_loop(0, steps, lambda i, c: (body(i), c)[1], 0)
            return
        v, half = 1 + lax.div(group, 2), lax.rem(group, 2)
        each = n // 2
        if steps < each:
            def many(i, c):
                for j in range(each):
                    @pl.when(1 + half * each + j < n)
                    def _():
                        send(v, 1 + half * each + j)
                return c
            lax.fori_loop(0, 1, many, 0)
            lax.fori_loop(0, steps, lambda i, c: (body(i), c)[1], 0)
            return

        def step(i, c):
            send(v, 1 + half * each + i)
            body(i)
            return c

        lax.fori_loop(0, each - 1, step, 0)

        @pl.when(half == 0)
        def _():
            send(v, each)

        lax.fori_loop(each - 1, steps, lambda i, c: (body(i), c)[1], 0)

    def taps_of(v, axis, flip):
        raw = [jnp.full((8, 128), kernels_ref[v, axis, t], F32) for t in range(TAPS)]
        whole = raw[0]
        for t in range(1, TAPS):
            whole = whole + raw[t]
        scale = 1.0 / whole
        taps = [r * scale for r in raw]
        return taps[::-1] if flip else taps

    def build(v, carry):
        raw = [kernels_ref[v, 2, t] for t in range(TAPS)]
        whole = jnp.full((1, 128), raw[0], F32)
        for t in range(1, TAPS):
            whole = whole + raw[t]
        scale = 1.0 / whole

        def banded(tap_at):
            band = jnp.zeros(tap_at.shape, F32)
            for t in range(TAPS):
                band = jnp.where(tap_at == t, raw[t], band)
            return split(band * scale)

        pair, lanes = lax.div(v, 2), pl.ds(pl.multiple_of(lax.rem(v, 2) * 128, 128), 128)
        row = lax.broadcasted_iota(jnp.int32, (128, 128), 0)
        col = lax.broadcasted_iota(jnp.int32, (128, 128), 1)
        high, low = banded(row - col + HALF)
        w_fore[pair, 0:128, lanes] = high
        w_fore[pair, 128:256, lanes] = high
        w_fore[pair, 256:384, lanes] = low
        high, low = banded(col - row + HALF)
        w_back[v, 0:128] = high
        w_back[v, 128:256] = high
        w_low[v] = low
        row = lax.broadcasted_iota(jnp.int32, (16, 128), 0)
        col = lax.broadcasted_iota(jnp.int32, (16, 128), 1)
        high, low = banded(jnp.where(row < 8, row - 8, row + 120) - col + HALF)
        w_side[v, 0:16] = high
        w_side[v, 16:32] = low
        w_fore[pair, 384:400, lanes] = high
        w_fore[pair, 400:416, lanes] = high
        w_fore[pair, 416:432, lanes] = low
        w_fore[pair, 432:512, lanes] = jnp.zeros((80, 128), BF16)
        return carry

    lax.fori_loop(0, views, build, 0)
    xed[0:8] = jnp.zeros((8, 16, 128), F32)
    xed[rows + 8:rows + 16] = jnp.zeros((8, 16, 128), F32)
    ratio[0:8] = jnp.zeros((8, 16, 128), F32)
    ratio[rows + 8:rows + 16] = jnp.zeros((8, 16, 128), F32)
    lined[0:16] = jnp.ones((16, 16, 128), F32)
    lined[rows + 16:rows + 32] = jnp.ones((16, 16, 128), F32)
    yed[:, 0:8] = jnp.zeros((rows, 8, 128), F32)
    yed[:, 24:32] = jnp.zeros((rows, 8, 128), F32)

    first, last = me == 0, me == n - 1
    front, rear = deep == 0, deep == depth - 1

    def widen(t, gone):
        high, low = split(jnp.where(gone, 0.0, field[t].reshape(slab, 128)))
        ends = []
        for side, face in ((0, front), (1, rear)):
            ends.append(jnp.where(jnp.logical_or(gone, face), 0.0, halo_z[side, t]))
        eh, el = split(jnp.concatenate(ends, axis=0))
        eh, el = eh.astype(F32), el.astype(F32)
        ends = jnp.concatenate([eh, el, eh, jnp.zeros((80, slab), F32)], axis=0).T
        wide[t, :, 0:128] = high
        wide[t, :, 128:256] = low
        wide[t, :, 256:384] = high
        wide[t, :, 384:512] = ends.astype(BF16)

    for copy in halos:
        copy.wait_recv()
    for t, gone in enumerate((first, False, False, last)):
        widen(t, gone)

    def along_y(taps, src, put, blocks):
        def block(b, carry):
            for t in range(2):
                sums = [None] * 8
                for r in range(22):
                    seen = src[b * 8 + 1 + r, pl.ds(t * 8, 8), :]
                    for j in range(max(0, r - 14), min(8, r + 1)):
                        term = taps[r - j] * seen
                        sums[j] = term if sums[j] is None else sums[j] + term
                for j in range(8):
                    put(b * 8 + j, t, sums[j])
            return carry

        lax.fori_loop(*blocks, block, 0)

    def forward(v, carry):
        part = lax.rem(v, 2)

        @pl.when(part == 0)
        def _():
            pair = lax.div(v, 2)

            def tile(t, c):
                res = dot(wide[t], w_fore[pair], NN)
                for p in range(2):
                    zed[p, :, pl.ds(pl.multiple_of(t * 8, 8), 8), :] = res[:, p * 128:p * 128 + 128].reshape(rows, 8, 128)
                return c

            lax.fori_loop(0, 4, tile, 0)

        taps = taps_of(v, 0, False)

        def along_x(i):
            for q in range(4):
                y = i * 4 + q
                low = high = None
                for o in range(1, 24):
                    seen = zed[part, y, pl.ds(o, 8), :]
                    if o <= 15:
                        term = taps[o - 1] * seen
                        low = term if low is None else low + term
                    if o >= 9:
                        term = taps[o - 9] * seen
                        high = term if high is None else high + term
                xed[y + 8, 0:8, :] = low
                xed[y + 8, 8:16, :] = high

        paced(v, along_x, rows // 4)

        def put(y, t, value):
            near = pl.reciprocal(value, approx=True)
            weights[v, y, pl.ds(t * 8, 8), :] = near * (2.0 - value * near)

        along_y(taps_of(v, 1, False), xed, put, (0, rows // 8))
        return carry

    lax.fori_loop(0, views, forward, 0)

    for copy in halos:
        copy.wait_send()

    def spill_chunk(c, side):
        at = pl.ds(pl.multiple_of(c * CHUNK, CHUNK), CHUNK)
        src, dst = total.at[0 if side == 0 else 3, at], got_x.at[1 - side, at]
        return pltpu.make_async_remote_copy(
            src_ref=src, dst_ref=dst, send_sem=chunk_send.at[side, c], recv_sem=chunk_recv.at[side, c],
            device_id=peer(SIDES[side]), device_id_type=MESH)

    def backward(v, group, final):
        shift = shift_ref[v]
        whole = tiles.at[v, pl.ds(0, n - 1)]
        pltpu.make_async_copy(whole, whole, a2a_recv.at[v]).wait()
        own(v, True)

        def line(d, c):
            for p in range(2):
                for t in range(2):
                    lined[16 + d * 2 + p, pl.ds(t * 8, 8), :] = tiles[v, d, pl.ds(p + t * 16, 8, stride=2), :]
            return c

        lax.fori_loop(0, n, line, 0, unroll=4)

        def divide(y, c):
            at = y + shift
            covered = jnp.logical_and(at >= 0, at < rows)
            ratio[y + 8] = jnp.where(covered, lined[at + 16] * weights[v, y], jnp.float32(1.0))
            return c

        lax.fori_loop(0, rows, divide, 0, unroll=8)

        def put(y, t, value):
            yed[y, pl.ds(8 + t * 8, 8), :] = value

        def along_x(taps, y, to):
            sums = [None] * 4
            for o in range(1, 24):
                seen = yed[y, pl.ds(o, 8), :]
                for j in range(4):
                    t = o + 7 - 8 * j
                    if 0 <= t < TAPS:
                        term = taps[t] * seen
                        sums[j] = term if sums[j] is None else sums[j] + term
            for j in range(4):
                spread[j, to] = sums[j]

        def finish_chunk(c):
            at = pl.ds(pl.multiple_of(c * CHUNK, CHUNK), CHUNK)
            lanes = pl.ds(pl.multiple_of(c * CHUNK * 8, CHUNK * 8), CHUNK * 8)
            src = spread[:, at] if not final else spread[:, 0:CHUNK]
            high, low = split(src.reshape(4 * CHUNK * 8, 128))
            res = dot(jnp.concatenate([high, low], axis=1), w_back[v], NN) + dot(high, w_low[v], NN)
            res = res.reshape(4, CHUNK, 8, 128)
            ends = dot(w_side[v], high, NT)
            ends = ends[0:16] + ends[16:32] + dot(w_side[v, 0:16], low, NT)
            for t in range(4):
                total[t, at] += res[t]
                for side in range(2):
                    spill[side, t, :, lanes] += ends[side * 8:side * 8 + 8, t * CHUNK * 8:(t + 1) * CHUNK * 8]

        if not final:
            along_y(taps_of(v, 1, True), ratio, put, (0, rows // 8))
            taps = taps_of(v, 0, True)

            def step(i):
                for q in range(4):
                    along_x(taps, i * 4 + q, i * 4 + q)

            paced(group, step, rows // 4)
            lax.fori_loop(0, chunks, lambda c, k: (finish_chunk(c), k)[1], 0)
            return

        def chunk(c, k):
            along_y(taps_of(v, 1, True), ratio, put, (c * (CHUNK // 8), (c + 1) * (CHUNK // 8)))
            taps = taps_of(v, 0, True)

            def step(i, kk):
                for q in range(4):
                    along_x(taps, c * CHUNK + i * 4 + q, i * 4 + q)
                return kk

            lax.fori_loop(0, CHUNK // 4, step, 0)
            finish_chunk(c)
            for side in range(2):
                spill_chunk(c, side).start()
            return k

        lax.fori_loop(0, chunks, chunk, 0)

    for t in range(4):
        total[t] = jnp.zeros((rows, 8, 128), F32)
        spill[0, t] = jnp.zeros((8, slab), F32)
        spill[1, t] = jnp.zeros((8, slab), F32)
    with_sends = 2 * (views - 1) - views
    lax.fori_loop(0, with_sends, lambda v, c: (backward(v, v + views, False), c)[1], 0)
    lax.fori_loop(with_sends, views - 1, lambda v, c: (backward(v, None, False), c)[1], 0)
    backward(views - 1, None, True)

    spills = []
    for i, (sx, sz) in enumerate(SIDES[2:]):
        mine, theirs = (0, 1) if sz < 0 else (1, 0)
        if sx == 0:
            src, dst = spill.at[mine, pl.ds(1, 2)], got_z.at[theirs, pl.ds(1, 2)]
        else:
            src = spill.at[mine, 0 if sx < 0 else 3]
            dst = got_z.at[theirs, 3 if sx < 0 else 0]
        spills.append(pltpu.make_async_remote_copy(
            src_ref=src, dst_ref=dst, send_sem=spill_send.at[i], recv_sem=spill_recv.at[i],
            device_id=peer((sx, sz)), device_id_type=MESH))
    for copy in spills:
        copy.start()
    for v in range(views):
        whole = tiles.at[v, pl.ds(0, n - 1)]
        pltpu.make_async_copy(whole, whole, a2a_send.at[v]).wait()
    for copy in spills:
        copy.wait_recv()

    lane = lax.broadcasted_iota(jnp.int32, (32, 128), 1)
    row = lax.broadcasted_iota(jnp.int32, (32, 128), 0) % 16
    place = jnp.where(lane == jnp.where(row < 8, row, row + 112), 1.0, 0.0).astype(BF16)

    def last_chunk(c, k):
        at = pl.ds(pl.multiple_of(c * CHUNK, CHUNK), CHUNK)
        lanes = pl.ds(pl.multiple_of(c * CHUNK * 8, CHUNK * 8), CHUNK * 8)
        for side in range(2):
            spill_chunk(c, side).wait_recv()
        for t in range(2):
            outer, edge = (0, first) if t == 0 else (1, last)
            corner = 0 if t == 0 else 3
            ends = []
            for side, face in ((0, front), (1, rear)):
                end = got_z[side, 1 + t, :, lanes] + jnp.where(edge, 0.0, got_z[side, corner, :, lanes])
                ends.append(jnp.where(face, 0.0, end))
            both = jnp.concatenate(split(jnp.concatenate(ends, axis=0)), axis=0)
            spilled = dot(both, place, TN).reshape(CHUNK, 8, 128)
            summed = total[1 + t, at] + jnp.where(edge, 0.0, got_x[outer, at]) + spilled
            done = field[1 + t, at] * (summed * (1.0 / views))
            for q in range(CHUNK):
                out_ref[pl.ds(t * 8 * rows + c * CHUNK + q, 8, stride=rows), :] = done[q]
        return k

    lax.fori_loop(0, chunks, last_chunk, 0)
    for copy in spills:
        copy.wait_send()
    for c in range(chunks):
        for side in range(2):
            spill_chunk(c, side).wait_send()


def local(n, depth, estimate, observed, kernels, view_shift):
    views, nx = observed.shape[:2]
    rows = estimate.shape[1]
    est = estimate.reshape(16 * rows, 128)
    obs = observed.reshape(views, 2 * nx, 128)
    dma = pltpu.SemaphoreType.DMA
    vmem = lambda *shape: pltpu.VMEM(shape, F32)
    half = lambda *shape: pltpu.VMEM(shape, BF16)
    out = pl.pallas_call(
        functools.partial(kernel, n, depth, views),
        out_shape=jax.ShapeDtypeStruct((16 * rows, 128), F32),
        in_specs=[
            pl.BlockSpec(memory_space=pltpu.SMEM),
            pl.BlockSpec(memory_space=pltpu.SMEM),
            pl.BlockSpec(memory_space=pl.ANY),
            pl.BlockSpec(memory_space=pl.ANY),
        ],
        out_specs=pl.BlockSpec(memory_space=pltpu.VMEM),
        scratch_shapes=[
            vmem(16 * rows, 128),
            vmem(views, n, 32, 128),
            vmem(rows + 32, 16, 128),
            vmem(4, rows, 8, 128),
            half(4, rows * 8, 512),
            vmem(2, 4, 8, rows * 8),
            vmem(2, rows, 32, 128),
            vmem(rows + 16, 16, 128),
            vmem(views, rows, 16, 128),
            vmem(rows + 16, 16, 128),
            vmem(rows, 32, 128),
            vmem(4, rows, 8, 128),
            vmem(4, rows, 8, 128),
            vmem(2, 4, 8, rows * 8),
            vmem(2, rows, 8, 128),
            vmem(2, 4, 8, rows * 8),
            half(views // 2, 512, 256),
            half(views, 256, 128),
            half(views, 128, 128),
            half(views, 32, 128),
            dma(()), dma((views,)), dma((views,)), dma((views,)),
            dma((8,)), dma((8,)), dma((6,)), dma((6,)),
            dma((2, rows // CHUNK)), dma((2, rows // CHUNK)),
        ],
        compiler_params=pltpu.CompilerParams(
            collective_id=0, has_side_effects=True, vmem_limit_bytes=56 * 2**20),
    )(kernels, view_shift, est, obs)
    return out.reshape(estimate.shape)


def solution(mesh):
    return jax.shard_map(
        functools.partial(local, mesh.shape["xy"], mesh.shape["gz"]),
        mesh=mesh,
        in_specs=(P("xy", None, "gz"), P(None, None, "xy", "gz"), P(), P()),
        out_specs=P("xy", None, "gz"),
        check_vma=False,
    )
```

time: 86.2 us -> 67 us (0.78)
  the two profiles are of different devices: /device:TPU:23 before, /device:TPU:1 now
where the time goes in v1:
time: 67 us; the launch traced here: 65.9 us
  Pallas kernels  64 us (96%)
  local copies, waits for them, and re-layouts  1.89 us (3%)
    pallas_call x1, Pallas kernels, local(): pl.pallas_call(functools.partial(kernel, n, depth, views), out_shape=jax....  64 us
    unnamed x1, local copies, waits for them, and re-layouts  1.89 us

profile of v1, /device:TPU:1, one launch (start us, length us, event | category | flops | bytes accessed | tf_op | source)
XLA Modules:
  0.0 65.9 jit_solution(3296381810069649195)
XLA Ops:
  0.0 64.0 %shard_map.46 = f32[1024,128]{1,0:T(8,128)} custom-call(f32[6,3,15]{2,1,0:T(4,128)} %kernels_ref.1, s32[6]{0:T(128)} %shift_ref.1, f32[1024,128]{1,0:T(8,128)} %bitcast.5, f32[6,1024,128]{2,1,0:T(8,128)} %bitcast.3), custom_call_target="tpu_custom_call" | custom-call | tf_op jit(solution)/shard_map/pallas_call | solution.py:431
  64.0 1.9 %copy.6 = f32[16,64,128]{2,1,0:T(8,128)} copy(f32[16,64,128]{2,1,0:T(8,128)} %bitcast.4) | data formatting | bytes 1048576

commit v2 on v1

--- a/solution.py
+++ b/solution.py
@@ -26,6 +26,8 @@
 NT = ((1,), (1,))
 TN = ((0,), (0,))
 CHUNK = 16
+STEPS = 8
+EARLY = 2
 
 
 def kernel(n, depth, views, kernels_ref, shift_ref, est_ref, obs_ref, out_ref,
@@ -93,49 +95,39 @@
     for copy in halos:
         copy.start()
 
-    def send(v, k):
-        to = lax.rem(me + k, n)
+    def send(v, i):
+        to = lax.rem(me + 1 + lax.rem(i * 13, n - 1), n)
         pltpu.make_async_remote_copy(
             src_ref=obs_ref.at[v, pl.ds(pl.multiple_of(to * 32, 32), 32)],
             dst_ref=tiles.at[v, me],
             send_sem=a2a_send.at[v], recv_sem=a2a_recv.at[v],
             device_id={"xy": to}, device_id_type=MESH).start()
 
-    def send_first(k, carry):
-        send(0, k)
-        return carry
-
-    lax.fori_loop(1, n, send_first, 0)
-
-    def paced(group, body, steps):
+    lax.fori_loop(0, n - 1, lambda i, c: (send(0, i), c)[1], 0)
+
+    def paced(group, body):
         if group is None:
-            lax.fori_loop(0, steps, lambda i, c: (body(i), c)[1], 0)
+            lax.fori_loop(0, STEPS, lambda i, c: (body(i), c)[1], 0)
             return
-        v, half = 1 + lax.div(group, 2), lax.rem(group, 2)
+        v, half = EARLY + lax.div(group, 2), lax.rem(group, 2)
         each = n // 2
-        if steps < each:
-            def many(i, c):
-                for j in range(each):
-                    @pl.when(1 + half * each + j < n)
-                    def _():
-                        send(v, 1 + half * each + j)
-                return c
-            lax.fori_loop(0, 1, many, 0)
-            lax.fori_loop(0, steps, lambda i, c: (body(i), c)[1], 0)
-            return
+        per = each // STEPS
 
         def step(i, c):
-            send(v, 1 + half * each + i)
+            for j in range(per):
+                send(v, half * each + i * per + j)
             body(i)
             return c
 
-        lax.fori_loop(0, each - 1, step, 0)
+        lax.fori_loop(0, STEPS - 1, step, 0)
+        for j in range(per - 1):
+            send(v, half * each + (STEPS - 1) * per + j)
 
         @pl.when(half == 0)
         def _():
-            send(v, each)
-
-        lax.fori_loop(each - 1, steps, lambda i, c: (body(i), c)[1], 0)
+            send(v, each - 1)
+
+        body(STEPS - 1)
 
     def taps_of(v, axis, flip):
         raw = [jnp.full((8, 128), kernels_ref[v, axis, t], F32) for t in range(TAPS)]
@@ -209,6 +201,7 @@
 
     for copy in halos:
         copy.wait_recv()
+    lax.fori_loop(0, n - 1, lambda i, c: (send(1, i), c)[1], 0)
     for t, gone in enumerate((first, False, False, last)):
         widen(t, gone)
 
@@ -234,19 +227,16 @@
         def _():
             pair = lax.div(v, 2)
 
-            def tile(t, c):
+            for t in range(4):
                 res = dot(wide[t], w_fore[pair], NN)
                 for p in range(2):
-                    zed[p, :, pl.ds(pl.multiple_of(t * 8, 8), 8), :] = res[:, p * 128:p * 128 + 128].reshape(rows, 8, 128)
-                return c
-
-            lax.fori_loop(0, 4, tile, 0)
+                    zed[p, :, t * 8:t * 8 + 8, :] = res[:, p * 128:p * 128 + 128].reshape(rows, 8, 128)
 
         taps = taps_of(v, 0, False)
 
         def along_x(i):
-            for q in range(4):
-                y = i * 4 + q
+            for q in range(rows // STEPS):
+                y = i * (rows // STEPS) + q
                 low = high = None
                 for o in range(1, 24):
                     seen = zed[part, y, pl.ds(o, 8), :]
@@ -259,7 +249,7 @@
                 xed[y + 8, 0:8, :] = low
                 xed[y + 8, 8:16, :] = high
 
-        paced(v, along_x, rows // 4)
+        paced(v, along_x)
 
         def put(y, t, value):
             near = pl.reciprocal(value, approx=True)
@@ -320,8 +310,7 @@
         def finish_chunk(c):
             at = pl.ds(pl.multiple_of(c * CHUNK, CHUNK), CHUNK)
             lanes = pl.ds(pl.multiple_of(c * CHUNK * 8, CHUNK * 8), CHUNK * 8)
-            src = spread[:, at] if not final else spread[:, 0:CHUNK]
-            high, low = split(src.reshape(4 * CHUNK * 8, 128))
+            high, low = split(spread[:, 0:CHUNK].reshape(4 * CHUNK * 8, 128))
             res = dot(jnp.concatenate([high, low], axis=1), w_back[v], NN) + dot(high, w_low[v], NN)
             res = res.reshape(4, CHUNK, 8, 128)
             ends = dot(w_side[v], high, NT)
@@ -331,16 +320,27 @@
                 for side in range(2):
                     spill[side, t, :, lanes] += ends[side * 8:side * 8 + 8, t * CHUNK * 8:(t + 1) * CHUNK * 8]
 
+        def finish_tile(t):
+            high, low = split(spread[t].reshape(slab, 128))
+            res = dot(jnp.concatenate([high, low], axis=1), w_back[v], NN) + dot(high, w_low[v], NN)
+            ends = dot(w_side[v], high, NT)
+            ends = ends[0:16] + ends[16:32] + dot(w_side[v, 0:16], low, NT)
+            total[t] += res.reshape(rows, 8, 128)
+            for side in range(2):
+                spill[side, t] += ends[side * 8:side * 8 + 8]
+
         if not final:
             along_y(taps_of(v, 1, True), ratio, put, (0, rows // 8))
             taps = taps_of(v, 0, True)
 
             def step(i):
-                for q in range(4):
-                    along_x(taps, i * 4 + q, i * 4 + q)
-
-            paced(group, step, rows // 4)
-            lax.fori_loop(0, chunks, lambda c, k: (finish_chunk(c), k)[1], 0)
+                for q in range(rows // STEPS):
+                    y = i * (rows // STEPS) + q
+                    along_x(taps, y, y)
+
+            paced(group, step)
+            for t in range(4):
+                finish_tile(t)
             return
 
         def chunk(c, k):
@@ -364,7 +364,7 @@
         total[t] = jnp.zeros((rows, 8, 128), F32)
         spill[0, t] = jnp.zeros((8, slab), F32)
         spill[1, t] = jnp.zeros((8, slab), F32)
-    with_sends = 2 * (views - 1) - views
+    with_sends = 2 * (views - EARLY) - views
     lax.fori_loop(0, with_sends, lambda v, c: (backward(v, v + views, False), c)[1], 0)
     lax.fori_loop(with_sends, views - 1, lambda v, c: (backward(v, None, False), c)[1], 0)
     backward(views - 1, None, True)
@@ -430,7 +430,7 @@
     half = lambda *shape: pltpu.VMEM(shape, BF16)
     out = pl.pallas_call(
         functools.partial(kernel, n, depth, views),
-        out_shape=jax.ShapeDtypeStruct((16 * rows, 128), F32),
+        out_shape=pltpu.VMEM((16 * rows, 128), F32),
         in_specs=[
             pl.BlockSpec(memory_space=pltpu.SMEM),
             pl.BlockSpec(memory_space=pltpu.SMEM),

time: 67 us -> 61.6 us (0.919); the launches traced: 65.9 us -> 61.4 us
  Pallas kernels: 64 us -> 60.6 us
  local copies, waits for them, and re-layouts: 1.89 us -> 0.8 us
    pallas_call x1, Pallas kernels: 64 us -> 60.6 us  [local(): pl.pallas_call(functools.partial(kernel, n, depth, views), out_shape=pltp...]
    unnamed x1, local copies, waits for them, and re-layouts: 1.89 us -> 0.8 us
where the time goes in v2:
time: 61.6 us; the launch traced here: 61.4 us
  Pallas kernels  60.6 us (98%)
  local copies, waits for them, and re-layouts  0.8 us (1%)
    pallas_call x1, Pallas kernels, local(): pl.pallas_call(functools.partial(kernel, n, depth, views), out_shape=pltp...  60.6 us

profile of v2, /device:TPU:1, one launch (start us, length us, event | category | flops | bytes accessed | tf_op | source)
XLA Modules:
  0.0 61.4 jit_solution(14743643117867482541)
XLA Ops:
  0.0 60.6 %shard_map.46 = f32[1024,128]{1,0:T(8,128)S(1)} custom-call(f32[6,3,15]{2,1,0:T(4,128)} %kernels_ref.1, s32[6]{0:T(128)} %shift_ref.1, f32[1024,128]{1,0:T(8,128)} %bitcast.5, f32[6,1024,128]{2,1,0:T(8,128)} %bitcast.4), custom_call_target="tpu_custom_call" | custom-call | tf_op jit(solution)/shard_map/pallas_call | solution.py:431
  60.6 0.8 %copy.6 = f32[16,64,128]{2,1,0:T(8,128)} copy(f32[16,64,128]{2,1,0:T(8,128)S(1)} %bitcast.3) | data formatting | bytes 1048576

commit v3 on v2

--- a/solution.py
+++ b/solution.py
@@ -30,8 +30,8 @@
 EARLY = 2
 
 
-def kernel(n, depth, views, kernels_ref, shift_ref, est_ref, obs_ref, out_ref,
-           est, tiles, lined, field, wide, halo_z, zed, xed, weights, ratio, yed, spread, total, spill,
+def kernel(n, depth, views, kernels_in, shift_in, est_ref, obs_ref, out_ref,
+           kernels_ref, shift_ref, small_sem, est, tiles, lined, field, wide, halo_z, zed, xed, weights, ratio, yed, spread, total, spill,
            got_x, got_z, w_fore, w_back, w_low, w_side,
            est_sem, a2a_send, a2a_recv, own_sem, halo_send, halo_recv, spill_send, spill_recv,
            chunk_send, chunk_recv):
@@ -39,9 +39,6 @@
     slab = rows * 8
     chunks = rows // CHUNK
     me, deep = lax.axis_index("xy"), lax.axis_index("gz")
-    load = pltpu.make_async_copy(est_ref, est, est_sem)
-    load.start()
-
     def peer(side):
         return {"xy": lax.rem(me + side[0] + n, n), "gz": lax.rem(deep + side[1] + depth, depth)}
 
@@ -51,9 +48,16 @@
         pl.semaphore_signal(barrier, inc=1, device_id={"xy": lax.rem(me + k, n)}, device_id_type=MESH)
         return carry
 
-    lax.fori_loop(1, n, greet, 0)
+    lax.fori_loop(1, n, greet, 0, unroll=31)
     for side in SIDES[2:]:
         pl.semaphore_signal(barrier, inc=1, device_id=peer(side), device_id_type=MESH)
+
+    load = pltpu.make_async_copy(est_ref, est, est_sem)
+    load.start()
+    small = (pltpu.make_async_copy(kernels_in, kernels_ref, small_sem.at[0]),
+             pltpu.make_async_copy(shift_in, shift_ref, small_sem.at[1]))
+    for copy in small:
+        copy.start()
 
     def own(v, wait):
         copy = pltpu.make_async_copy(
@@ -173,6 +177,8 @@
         w_fore[pair, 432:512, lanes] = jnp.zeros((80, 128), BF16)
         return carry
 
+    for copy in small:
+        copy.wait()
     lax.fori_loop(0, views, build, 0)
     xed[0:8] = jnp.zeros((8, 16, 128), F32)
     xed[rows + 8:rows + 16] = jnp.zeros((8, 16, 128), F32)
@@ -432,13 +438,16 @@
         functools.partial(kernel, n, depth, views),
         out_shape=pltpu.VMEM((16 * rows, 128), F32),
         in_specs=[
-            pl.BlockSpec(memory_space=pltpu.SMEM),
-            pl.BlockSpec(memory_space=pltpu.SMEM),
+            pl.BlockSpec(memory_space=pl.ANY),
+            pl.BlockSpec(memory_space=pl.ANY),
             pl.BlockSpec(memory_space=pl.ANY),
             pl.BlockSpec(memory_space=pl.ANY),
         ],
         out_specs=pl.BlockSpec(memory_space=pltpu.VMEM),
         scratch_shapes=[
+            pltpu.SMEM(kernels.shape, F32),
+            pltpu.SMEM((views,), jnp.int32),
+            dma((2,)),
             vmem(16 * rows, 128),
             vmem(views, n, 32, 128),
             vmem(rows + 32, 16, 128),

time: 61.6 us -> 60.4 us (0.981)
  Pallas kernels: 60.6 us -> 59.5 us
    pallas_call x1, Pallas kernels: 60.6 us -> 59.5 us  [local(): pl.pallas_call(functools.partial(kernel, n, depth, views), out_shape=pltp...]
where the time goes in v3:
time: 60.4 us; the launch traced here: 60.3 us
  Pallas kernels  59.5 us (99%)
  local copies, waits for them, and re-layouts  0.8 us (1%)
    pallas_call x1, Pallas kernels, local(): pl.pallas_call(functools.partial(kernel, n, depth, views), out_shape=pltp...  59.5 us

profile of v3, /device:TPU:1, one launch (start us, length us, event | category | flops | bytes accessed | tf_op | source)
XLA Modules:
  0.0 60.3 jit_solution(5593099188612458664)
XLA Ops:
  0.0 59.5 %shard_map.46 = f32[1024,128]{1,0:T(8,128)S(1)} custom-call(f32[6,3,15]{2,1,0:T(4,128)} %kernels_in.1, s32[6]{0:T(128)} %shift_in.1, f32[1024,128]{1,0:T(8,128)} %bitcast.5, f32[6,1024,128]{2,1,0:T(8,128)} %bitcast.4), custom_call_target="tpu_custom_call" | custom-call | tf_op jit(solution)/shard_map/pallas_call | solution.py:437
  59.5 0.8 %copy.6 = f32[16,64,128]{2,1,0:T(8,128)} copy(f32[16,64,128]{2,1,0:T(8,128)S(1)} %bitcast.3) | data formatting | bytes 1048576

commit v4 on v3

--- a/solution.py
+++ b/solution.py
@@ -48,9 +48,9 @@
         pl.semaphore_signal(barrier, inc=1, device_id={"xy": lax.rem(me + k, n)}, device_id_type=MESH)
         return carry
 
-    lax.fori_loop(1, n, greet, 0, unroll=31)
     for side in SIDES[2:]:
         pl.semaphore_signal(barrier, inc=1, device_id=peer(side), device_id_type=MESH)
+    lax.fori_loop(1, n, greet, 0, unroll=31)
 
     load = pltpu.make_async_copy(est_ref, est, est_sem)
     load.start()
@@ -276,6 +276,17 @@
             src_ref=src, dst_ref=dst, send_sem=chunk_send.at[side, c], recv_sem=chunk_recv.at[side, c],
             device_id=peer(SIDES[side]), device_id_type=MESH)
 
+    spills = []
+    for i, (sx, sz) in enumerate(SIDES[2:]):
+        mine, theirs = (0, 1) if sz < 0 else (1, 0)
+        if sx == 0:
+            src, dst = spill.at[mine, pl.ds(1, 2)], got_z.at[theirs, pl.ds(1, 2)]
+        else:
+            src = spill.at[mine, 0 if sx < 0 else 3]
+            dst = got_z.at[theirs, 3 if sx < 0 else 0]
+        spills.append(pltpu.make_async_remote_copy(
+            src_ref=src, dst_ref=dst, send_sem=spill_send.at[i], recv_sem=spill_recv.at[i],
+            device_id=peer((sx, sz)), device_id_type=MESH))
     def backward(v, group, final):
         shift = shift_ref[v]
         whole = tiles.at[v, pl.ds(0, n - 1)]
@@ -360,6 +371,12 @@
 
             lax.fori_loop(0, CHUNK // 4, step, 0)
             finish_chunk(c)
+
+            @pl.when(c == chunks - 1)
+            def _():
+                for copy in spills:
+                    copy.start()
+
             for side in range(2):
                 spill_chunk(c, side).start()
             return k
@@ -375,19 +392,6 @@
     lax.fori_loop(with_sends, views - 1, lambda v, c: (backward(v, None, False), c)[1], 0)
     backward(views - 1, None, True)
 
-    spills = []
-    for i, (sx, sz) in enumerate(SIDES[2:]):
-        mine, theirs = (0, 1) if sz < 0 else (1, 0)
-        if sx == 0:
-            src, dst = spill.at[mine, pl.ds(1, 2)], got_z.at[theirs, pl.ds(1, 2)]
-        else:
-            src = spill.at[mine, 0 if sx < 0 else 3]
-            dst = got_z.at[theirs, 3 if sx < 0 else 0]
-        spills.append(pltpu.make_async_remote_copy(
-            src_ref=src, dst_ref=dst, send_sem=spill_send.at[i], recv_sem=spill_recv.at[i],
-            device_id=peer((sx, sz)), device_id_type=MESH))
-    for copy in spills:
-        copy.start()
     for v in range(views):
         whole = tiles.at[v, pl.ds(0, n - 1)]
         pltpu.make_async_copy(whole, whole, a2a_send.at[v]).wait()

time: 60.4 us -> 60 us (level)
  no operation moved by 1% of the time
where the time goes in v4:
time: 60 us; the launch traced here: 59.9 us
  Pallas kernels  59.1 us (98%)
  local copies, waits for them, and re-layouts  0.8 us (1%)
    pallas_call x1, Pallas kernels, local(): pl.pallas_call(functools.partial(kernel, n, depth, views), out_shape=pltp...  59.1 us

profile of v4, /device:TPU:1, one launch (start us, length us, event | category | flops | bytes accessed | tf_op | source)
XLA Modules:
  0.0 59.9 jit_solution(14179358493021011283)
XLA Ops:
  0.0 59.1 %shard_map.46 = f32[1024,128]{1,0:T(8,128)S(1)} custom-call(f32[6,3,15]{2,1,0:T(4,128)} %kernels_in.1, s32[6]{0:T(128)} %shift_in.1, f32[1024,128]{1,0:T(8,128)} %bitcast.5, f32[6,1024,128]{2,1,0:T(8,128)} %bitcast.4), custom_call_target="tpu_custom_call" | custom-call | tf_op jit(solution)/shard_map/pallas_call | solution.py:441
  59.1 0.8 %copy.6 = f32[16,64,128]{2,1,0:T(8,128)} copy(f32[16,64,128]{2,1,0:T(8,128)S(1)} %bitcast.3) | data formatting | bytes 1048576

commit v5 on v4

--- a/solution.py
+++ b/solution.py
@@ -100,7 +100,7 @@
         copy.start()
 
     def send(v, i):
-        to = lax.rem(me + 1 + lax.rem(i * 13, n - 1), n)
+        to = lax.bitwise_xor(me, 1 + lax.rem(i * 13, n - 1))
         pltpu.make_async_remote_copy(
             src_ref=obs_ref.at[v, pl.ds(pl.multiple_of(to * 32, 32), 32)],
             dst_ref=tiles.at[v, me],

time: 60 us -> 59.7 us (level)
  no operation moved by 1% of the time
where the time goes in v5:
time: 59.7 us; the launch traced here: 59.6 us
  Pallas kernels  58.8 us (98%)
  local copies, waits for them, and re-layouts  0.8 us (1%)
    pallas_call x1, Pallas kernels, local(): pl.pallas_call(functools.partial(kernel, n, depth, views), out_shape=pltp...  58.8 us

profile of v5, /device:TPU:1, one launch (start us, length us, event | category | flops | bytes accessed | tf_op | source)
XLA Modules:
  0.0 59.6 jit_solution(7481334216289149410)
XLA Ops:
  0.0 58.8 %shard_map.46 = f32[1024,128]{1,0:T(8,128)S(1)} custom-call(f32[6,3,15]{2,1,0:T(4,128)} %kernels_in.1, s32[6]{0:T(128)} %shift_in.1, f32[1024,128]{1,0:T(8,128)} %bitcast.5, f32[6,1024,128]{2,1,0:T(8,128)} %bitcast.4), custom_call_target="tpu_custom_call" | custom-call | tf_op jit(solution)/shard_map/pallas_call | solution.py:441
  58.8 0.8 %copy.6 = f32[16,64,128]{2,1,0:T(8,128)} copy(f32[16,64,128]{2,1,0:T(8,128)S(1)} %bitcast.3) | data formatting | bytes 1048576
